TPU v7x, 128 devices: a whole 4x4x4 slice. The times are simulated.
128 devices in a mesh: gx: 8 (over z, core), gy: 16 (over x, y).
Axes of the slice: x: 4, y: 4, z: 4, core: 2. Of those that a mesh axis runs over, the one named last changes fastest.
Arguments:
- features: bfloat16 [8, 16, 16, 8, 8, 8, 128], P('gx', 'gy'), may hold values from -6 to 6
- cotangent: bfloat16 [8, 16, 16, 8, 8, 8, 128], P('gx', 'gy'), may hold values from -6 to 6
- kernel_weight: bfloat16 [3, 3, 3, 128, 128], replicated, may hold values from -0.109375 to 0.109375
- conv_bias: float32 [128], replicated, may hold values from -3 to 3
- send_lists: int32 [8, 16, 8, 4], P('gx', 'gy'), may hold values from 0 to 16, as said below
- kernel_map: int32 [8, 16, 16, 27], P('gx', 'gy'), may hold values from 0 to 48, as said below
Outputs:
- activated: bfloat16 [8, 16, 16, 8, 8, 8, 128], P('gx', 'gy')
- input_grad: bfloat16 [8, 16, 16, 8, 8, 8, 128], P('gx', 'gy')
- weight_grad: float32 [3, 3, 3, 128, 128], replicated
- bias_grad: float32 [128], replicated
Inputs may be any that keep to these rules, and one draw needn't show every extreme that they name: send_lists[i, j, k] names distinct own bricks (0 to 15) in its first 1 to 4 slots and 16 in the rest; it is all 16 where region (i+dx, j+dy) of direction k lies outside the grid. In every draw some interior region receives 4 named bricks in all 8 lists that reach it. kernel_map[i, j, b, 13] = b. Other entries name an own brick (below 16), a received slot 16 + 4 k + r whose brick is named (r below the count named in the list k of region (i-dx, j-dy)), or 48, an absent brick. Every named received slot appears somewhere in the region's map.
All inputs are finite; a program needn't handle non-finite values.
Results may differ from a plain program's by a relative error of at most 0.008.
Values may be sent and summed in bfloat16 or wider, within the bound.
A program may use at most 128 MiB of HBM per device.

v0:
```python
import math
import jax
import jax.numpy as jnp
import numpy as np
from jax import lax
from jax.sharding import PartitionSpec as P

DIRECTIONS = ((-1, -1), (-1, 0), (-1, 1), (0, -1), (0, 1), (1, -1), (1, 0), (1, 1))


def passed_along(block, axis, distance):
    devices = range(lax.axis_size(axis))
    route = [(i - distance, i) for i in devices if i - distance in devices]
    return lax.ppermute(block, axis, route)


def brick_faces(bricks):
    last_idx = bricks.shape[1] - 1
    return jnp.stack(
        [
            bricks[:, 0],
            bricks[:, last_idx],
            bricks[:, :, 0],
            bricks[:, :, last_idx],
            bricks[:, :, :, 0],
            bricks[:, :, :, last_idx],
        ],
        axis=1,
    )


def sign_of(coord, edge_len):
    if coord == 0:
        return -1
    if coord == edge_len + 1:
        return 1
    return 0


def face_index(sign_val, coord, edge_len):
    if sign_val < 0:
        return edge_len - 1
    if sign_val > 0:
        return 0
    return coord - 1


def rim_tables(edge_len):
    side = edge_len + 2
    cells = side * side * side
    centre_mask = np.zeros((cells,), np.bool_)
    offset_col = np.zeros((cells,), np.int32)
    inner_pos = np.zeros((cells,), np.int32)
    face_pos = np.zeros((cells,), np.int32)
    square = edge_len * edge_len
    for cell in range(cells):
        p, q, r = (cell // (side * side), cell // side % side, cell % side)
        a, b, c = (sign_of(p, edge_len), sign_of(q, edge_len), sign_of(r, edge_len))
        offset_col[cell] = 9 * (a + 1) + 3 * (b + 1) + (c + 1)
        if a == 0 and b == 0 and (c == 0):
            centre_mask[cell] = True
            inner_pos[cell] = ((p - 1) * edge_len + (q - 1)) * edge_len + (r - 1)
            continue
        if a != 0:
            face_id = 1 if a < 0 else 0
            first, second = (face_index(b, q, edge_len), face_index(c, r, edge_len))
        elif b != 0:
            face_id = 3 if b < 0 else 2
            first, second = (p - 1, face_index(c, r, edge_len))
        else:
            face_id = 5 if c < 0 else 4
            first, second = (p - 1, q - 1)
        face_pos[cell] = face_id * square + first * edge_len + second
    return (centre_mask, offset_col, inner_pos, face_pos)


def assemble(volume, face_table, brick_map):
    brick_count = volume.shape[0]
    edge_len = volume.shape[1]
    channels = volume.shape[4]
    side = edge_len + 2
    cube = edge_len * edge_len * edge_len
    square = edge_len * edge_len
    centre_mask, offset_col, inner_pos, face_pos = rim_tables(edge_len)
    entries = jnp.take(brick_map, jnp.asarray(offset_col), axis=1).astype(jnp.int32)
    brick_ids = jnp.arange(brick_count, dtype=jnp.int32)[:, None]
    own_rows = brick_ids * cube + jnp.asarray(inner_pos)[None, :]
    rim_rows = brick_count * cube + entries * (6 * square) + jnp.asarray(face_pos)[None, :]
    row_ids = jnp.where(jnp.asarray(centre_mask)[None, :], own_rows, rim_rows).astype(jnp.int32)
    pool = jnp.concatenate([volume.reshape(-1, channels), face_table.reshape(-1, channels)], axis=0)
    gathered = jnp.take(pool, row_ids.reshape(-1), axis=0)
    return gathered.reshape(brick_count, side, side, side, channels)


def conv_valid(padded, kernel):
    return lax.conv_general_dilated(
        padded,
        kernel,
        (1, 1, 1),
        "VALID",
        dimension_numbers=("NDHWC", "DHWIO", "NDHWC"),
        preferred_element_type=jnp.float32,
    )


def weight_terms(padded, slope_grad):
    edge_len = slope_grad.shape[1]
    channels = slope_grad.shape[4]
    flat_slope = slope_grad.reshape(-1, channels)
    partials = []
    for o in range(27):
        a, b, c = (o // 9, o // 3 % 3, o % 3)
        window = padded[:, a : a + edge_len, b : b + edge_len, c : c + edge_len].reshape(
            -1, channels
        )
        partials.append(
            lax.dot_general(
                window, flat_slope, (((0,), (0,)), ((), ())), preferred_element_type=jnp.float32
            )
        )
    return jnp.stack(partials).reshape(3, 3, 3, channels, channels)


def deliver(outgoing):
    columns_count = lax.axis_size("gy")
    arrived = []
    for k in range(8):
        shift_by = DIRECTIONS[k][0] * columns_count + DIRECTIONS[k][1]
        arrived.append(passed_along(outgoing[k], ("gx", "gy"), shift_by))
    return jnp.stack(arrived)


def neighbour_table(volume, send_list):
    own_faces = brick_faces(volume)
    face_shape = own_faces.shape[1:]
    source = jnp.concatenate([volume, jnp.zeros((1,) + volume.shape[1:], volume.dtype)], axis=0)
    arrived = deliver(source[send_list])
    incoming = brick_faces(arrived.reshape((-1,) + volume.shape[1:]))
    return jnp.concatenate(
        [own_faces, incoming, jnp.zeros((1,) + face_shape, own_faces.dtype)], axis=0
    )


def shards(features, cotangent, kernel_weight, conv_bias, send_lists, kernel_map):
    volume = features[0, 0]
    send_list = send_lists[0, 0]
    brick_map = kernel_map[0, 0]
    padded = assemble(volume, neighbour_table(volume, send_list), brick_map)
    linear = conv_valid(padded, kernel_weight) + conv_bias
    logistic = jax.nn.sigmoid(linear)
    activated = (linear * logistic).astype(jnp.bfloat16)
    slope_grad = (
        cotangent[0, 0].astype(jnp.float32) * logistic * (1.0 + linear * (1.0 - logistic))
    ).astype(jnp.bfloat16)
    grad_padded = assemble(slope_grad, neighbour_table(slope_grad, send_list), brick_map)
    flipped = jnp.transpose(kernel_weight[::-1, ::-1, ::-1], (0, 1, 2, 4, 3))
    input_grad = conv_valid(grad_padded, flipped).astype(jnp.bfloat16)
    weight_part = weight_terms(padded, slope_grad)
    bias_part = jnp.sum(slope_grad, axis=(0, 1, 2, 3), dtype=jnp.float32)
    weight_total, bias_total = lax.psum((weight_part, bias_part), ("gx", "gy"))
    edge_len = volume.shape[1]
    total_voxels = (
        lax.axis_size("gx") * lax.axis_size("gy") * volume.shape[0] * edge_len * edge_len * edge_len
    )
    factor = 1.0 / math.sqrt(total_voxels)
    return (
        activated[None, None],
        input_grad[None, None],
        weight_total * factor,
        bias_total * factor,
    )


def solution(mesh):
    return jax.shard_map(
        shards,
        mesh=mesh,
        in_specs=(
            P("gx", "gy", None, None, None, None, None),
            P("gx", "gy", None, None, None, None, None),
            P(),
            P(),
            P("gx", "gy", None, None),
            P("gx", "gy", None, None),
        ),
        out_specs=(
            P("gx", "gy", None, None, None, None, None),
            P("gx", "gy", None, None, None, None, None),
            P(),
            P(),
        ),
        check_vma=False,
    )
```

profile of v0, /device:TPU:1, one launch (start us, length us, event | category | flops | bytes accessed | tf_op | source)
XLA Modules:
  0.0 490.1 jit_solution(15078585050110940367)
XLA Ops:
  7.2 2.2 copy.277
  9.6 2.0 concatenate.18
  11.7 4.7 gather_fusion
  16.4 4.5 fusion.54
  22.4 3.3 collective-permute-start.1
  25.7 2.6 collective-permute-start.2
  28.3 5.6 %collective-permute-start.3 = (bf16[4,8,8,8,128]{4,2,1,3,0:T(8,128)(2,1)}, bf16[4,8,8,8,128]{4,2,1,3,0:T(8,128)(2,1)}, u32[]{:S(2)}, u32[]{:S(2)}) collective-permute-start(bf16[4,8,8,8,128]{4,2,1,3,0:T(8,128)(2,1)} %get-tuple-element.43), channel_id=1, source_target_pairs={{1,0},{2,1},{3,2},{4,3},{5,4},{6,5},{7,6},{8,7},{9,8},{10,9},{11,1... | collective-permute-start | bytes 1572872 | tf_op jit(solution)/shard_map/ppermute | solution.py:14
  33.9 1.9 collective-permute-start.4
  36.8 1.8 fusion.55
  38.6 4.0 gather_fusion.2
  42.6 2.5 fusion.42
  45.1 1.8 copy.159
  54.5 9.5 %collective-permute-start.5 = (bf16[4,8,8,8,128]{4,2,1,3,0:T(8,128)(2,1)S(1)}, bf16[4,8,8,8,128]{4,2,1,3,0:T(8,128)(2,1)S(1)}, u32[]{:S(2)}, u32[]{:S(2)}) collective-permute-start(bf16[4,8,8,8,128]{4,2,1,3,0:T(8,128)(2,1)S(1)} %copy-done.10), channel_id=1, source_target_pairs={{0,15},{1,16},{2,17},{3,18},{4,19},{5,20},{6,21},{7,22},{8,23},{9,... | collective-permute-start | bytes 1572872 | tf_op jit(solution)/shard_map/ppermute | solution.py:14
  65.2 7.3 %collective-permute-start.6 = (bf16[4,8,8,8,128]{4,2,1,3,0:T(8,128)(2,1)S(1)}, bf16[4,8,8,8,128]{4,2,1,3,0:T(8,128)(2,1)S(1)}, u32[]{:S(2)}, u32[]{:S(2)}) collective-permute-start(bf16[4,8,8,8,128]{4,2,1,3,0:T(8,128)(2,1)S(1)} %copy-done.9), channel_id=1, source_target_pairs={{0,16},{1,17},{2,18},{3,19},{4,20},{5,21},{6,22},{7,23},{8,24},{9,... | collective-permute-start | bytes 1572872 | tf_op jit(solution)/shard_map/ppermute | solution.py:14
  78.7 5.6 %collective-permute-done.7 = bf16[4,8,8,8,128]{4,2,1,3,0:T(8,128)(2,1)S(1)} collective-permute-done((bf16[4,8,8,8,128]{4,2,1,3,0:T(8,128)(2,1)S(1)}, bf16[4,8,8,8,128]{4,2,1,3,0:T(8,128)(2,1)S(1)}, u32[]{:S(2)}, u32[]{:S(2)}) %collective-permute-start.7) | collective-permute-done | bytes 524320 | tf_op jit(solution)/shard_map/ppermute | solution.py:14
  84.7 2.4 fusion.52
  88.0 2.1 maximum_maximum_fusion
  90.1 25.3 %pad_maximum_fusion = bf16[27008,128]{1,0:T(8,128)(2,1)} fusion(bf16[18816,128]{1,0:T(8,128)(2,1)S(1)} %bitcast.412, bf16[8192,128]{1,0:T(8,128)(2,1)S(1)} %bitcast.420), kind=kLoop, calls=%fused_computation.5 | loop fusion | flops 13828096 | bytes 13828096 | tf_op jit(solution)/shard_map/concatenate | solution.py:90
  115.4 34.3 %gather_fusion.3 = bf16[16000,128]{1,0:T(8,128)(2,1)} fusion(bf16[27008,128]{1,0:T(8,128)(2,1)} %pad_maximum_fusion, s32[16384]{0:T(1024)S(1)} %pad_clamp_fusion), kind=kCustom, calls=%fused_computation.1.clone | custom fusion | bytes 8256000 | tf_op jit(solution)/shard_map/jit(_take)/gather | solution.py:91
  149.7 11.8 %broadcast_select_fusion.1 = bf16[16000,128]{1,0:T(8,128)(2,1)} fusion(bf16[16000,128]{1,0:T(8,128)(2,1)} %gather_fusion.3, pred[16000]{0:T(1024)(128)(4,1)S(1)} %compare_and_fusion), kind=kLoop, calls=%fused_computation.18 | loop fusion | flops 2048000 | bytes 8208000 | tf_op jit(solution)/shard_map/jit(_take)/select_n | solution.py:91
  161.6 8.7 %reshape.121 = bf16[16,10,10,10,128]{4,3,2,1,0:T(8,128)(2,1)} reshape(bf16[16000,128]{1,0:T(8,128)(2,1)} %broadcast_select_fusion.1) | data formatting | bytes 8192000 | tf_op jit(solution)/shard_map/reshape | solution.py:92
  170.2 7.7 %copy.173 = bf16[16,10,10,10,128]{4,0,3,2,1:T(8,128)(2,1)S(1)} copy(bf16[16,10,10,10,128]{4,3,2,1,0:T(8,128)(2,1)} %reshape.121) | data formatting | bytes 8192000 | tf_op jit(solution)/shard_map/reshape | solution.py:92
  178.0 18.6 %convert_reduce_fusion = (f32[128]{0:T(128)}, bf16[16,8,8,8,128]{4,0,3,2,1:T(8,128)(2,1)S(1)}, bf16[1,1,16,8,8,8,128]{6,2,5,4,3,1,0:T(8,128)(2,1)}) fusion(f32[128]{0:T(128)S(1)} %copy-done.28, bf16[1,1,16,8,8,8,128]{6,5,4,3,2,1,0:T(8,128)(2,1)S(1)} %copy-done.27, bf16[16,10,10,10,128]{4,0,3,2,1:T(8,128)(2,1)S(1)} %copy.173, ...), kind=kOutput, calls=%fused_computation.12 | convolution fusion | flops 7263485952 | bytes 11273216 | tf_op jit(solution)/shard_map/conv_general_dilated | solution.py:96
  198.1 1.9 copy.175
  222.0 1.8 slice_dynamic-update-slice_fusion.2
  227.2 2.0 concatenate.21.clone
  229.2 4.8 gather_fusion.1
  234.0 4.4 fusion.51
  241.4 1.9 collective-permute-start.9
  245.0 1.9 collective-permute-start.10
  246.9 85.8 %psum.15 = f32[128]{0:T(128)S(1)} all-reduce(f32[128]{0:T(128)S(1)} %copy-done.29), channel_id=1, replica_groups=mesh['gx'=8,'gy'=16] {'gx','gy'}, use_global_device_ids=true, to_apply=%region_2.5 | all-reduce | flops 128 | bytes 1024 | tf_op jit(solution)/shard_map/psum | solution.py:160
  333.2 2.1 copy.184
  335.3 5.1 %collective-permute-start.11 = (bf16[4,8,8,8,128]{4,3,2,1,0:T(8,128)(2,1)S(1)}, bf16[4,8,8,8,128]{4,3,2,1,0:T(8,128)(2,1)S(1)}, u32[]{:S(2)}, u32[]{:S(2)}) collective-permute-start(bf16[4,8,8,8,128]{4,3,2,1,0:T(8,128)(2,1)S(1)} %copy-done.14), channel_id=1, source_target_pairs={{1,0},{2,1},{3,2},{4,3},{5,4},{6,5},{7,6},{8,7},{9,8},{10,9},{11,1... | collective-permute-start | bytes 1572872 | tf_op jit(solution)/shard_map/ppermute | solution.py:14
  340.4 2.1 collective-permute-start.12
  342.5 1.9 copy.213
  344.4 7.3 %collective-permute-start.13 = (bf16[4,8,8,8,128]{4,3,2,1,0:T(8,128)(2,1)S(1)}, bf16[4,8,8,8,128]{4,3,2,1,0:T(8,128)(2,1)S(1)}, u32[]{:S(2)}, u32[]{:S(2)}) collective-permute-start(bf16[4,8,8,8,128]{4,3,2,1,0:T(8,128)(2,1)S(1)} %copy-done.12), channel_id=1, source_target_pairs={{0,15},{1,16},{2,17},{3,18},{4,19},{5,20},{6,21},{7,22},{8,23},{9,... | collective-permute-start | bytes 1572872 | tf_op jit(solution)/shard_map/ppermute | solution.py:14
  352.8 1.9 collective-permute-start.14
  358.4 2.0 collective-permute-done.12
  360.5 2.9 collective-permute-done.13
  363.5 13.8 %collective-permute-done.14 = bf16[4,8,8,8,128]{4,3,2,1,0:T(8,128)(2,1)S(1)} collective-permute-done((bf16[4,8,8,8,128]{4,3,2,1,0:T(8,128)(2,1)S(1)}, bf16[4,8,8,8,128]{4,3,2,1,0:T(8,128)(2,1)S(1)}, u32[]{:S(2)}, u32[]{:S(2)}) %collective-permute-start.14) | collective-permute-done | bytes 524320 | tf_op jit(solution)/shard_map/ppermute | solution.py:14
  377.4 2.2 fusion.50
  380.9 25.4 %pad_maximum_fusion.1 = bf16[27008,128]{1,0:T(8,128)(2,1)} fusion(bf16[18816,128]{1,0:T(8,128)(2,1)S(1)} %bitcast.411, bf16[8192,128]{1,0:T(8,128)(2,1)S(1)} %bitcast.418), kind=kLoop, calls=%fused_computation.6 | loop fusion | flops 13828096 | bytes 13828096 | tf_op jit(solution)/shard_map/concatenate | solution.py:90
  406.2 34.3 %gather_fusion.4 = bf16[16000,128]{1,0:T(8,128)(2,1)} fusion(bf16[27008,128]{1,0:T(8,128)(2,1)} %pad_maximum_fusion.1, s32[16384]{0:T(1024)S(1)} %copy-done.7), kind=kCustom, calls=%fused_computation.2.clone | custom fusion | bytes 8256000 | tf_op jit(solution)/shard_map/jit(_take)/gather | solution.py:91
  440.5 11.8 %broadcast_select_fusion = bf16[16000,128]{1,0:T(8,128)(2,1)} fusion(bf16[16000,128]{1,0:T(8,128)(2,1)} %gather_fusion.4, pred[16000]{0:T(1024)(128)(4,1)S(1)} %copy-done.16), kind=kLoop, calls=%fused_computation.17 | loop fusion | flops 2048000 | bytes 8208000 | tf_op jit(solution)/shard_map/jit(_take)/select_n | solution.py:91
  452.4 8.3 %reshape.126 = bf16[16,10,10,10,128]{4,3,2,1,0:T(8,128)(2,1)} reshape(bf16[16000,128]{1,0:T(8,128)(2,1)} %broadcast_select_fusion) | data formatting | bytes 8192000 | tf_op jit(solution)/shard_map/reshape | solution.py:92
  460.6 17.6 %convert_bitcast_fusion = bf16[1,1,16,8,8,8,128]{6,2,5,4,3,1,0:T(8,128)(2,1)S(1)} fusion(bf16[3,3,3,128,128]{4,3,2,1,0:T(8,128)(2,1)S(1)} %copy-done, bf16[16,10,10,10,128]{4,3,2,1,0:T(8,128)(2,1)} %reshape.126), kind=kOutput, calls=%fused_computation.20 | convolution fusion | flops 7248805888 | bytes 7077888 | tf_op jit(solution)/shard_map/conv_general_dilated | solution.py:96
  478.2 1.9 copy.214
  480.1 2.9 broadcast_multiply_fusion
  (160 shorter events, 56.7 us)
Async XLA Ops:
  7.2 170.8 %copy-start = (bf16[3,3,3,128,128]{4,3,2,1,0:T(8,128)(2,1)S(1)}, bf16[3,3,3,128,128]{4,3,2,1,0:T(8,128)(2,1)}, u32[]{:S(2)}) copy-start(bf16[3,3,3,128,128]{4,3,2,1,0:T(8,128)(2,1)} %param.20) | copy-start | bytes 2654212
  7.2 2.3 copy-start.25
  7.2 472.9 %all-reduce.4.cloned.1.call-start = ((), (), s32[]{:S(2)}) async-start(), calls=%async_computation | async-start | bytes 3538944 | tf_op jit(solution)/shard_map/psum | solution.py:160
  9.5 2.2 copy-start.22
  11.7 4.7 copy-start.17
  20.9 17.6 %copy-start.19 = (s32[1,1,16,27]{3,2,1,0:T(8,128)S(1)}, s32[1,1,16,27]{3,2,1,0:T(8,128)}, u32[]{:S(2)}) copy-start(s32[1,1,16,27]{3,2,1,0:T(8,128)} %param.23) | copy-start | bytes 5188
  20.9 21.7 %copy-start.20 = (s32[1000]{0:T(1024)S(1)}, s32[1000]{0:T(1024)}, u32[]{:S(2)}) copy-start(s32[1000]{0:T(1024)} %constant.18.clone) | copy-start | bytes 12004
  20.9 21.7 %copy-start.21 = (s32[1000]{0:T(1024)S(1)}, s32[1000]{0:T(1024)}, u32[]{:S(2)}) copy-start(s32[1000]{0:T(1024)} %constant.19.clone) | copy-start | bytes 12004
  20.9 21.7 %copy-start.26 = (pred[1000]{0:T(1024)(128)(4,1)S(1)}, pred[1000]{0:T(1024)(128)(4,1)}, u32[]{:S(2)}) copy-start(pred[1000]{0:T(1024)(128)(4,1)} %constant.20.clone) | copy-start | bytes 3004
  20.9 33.6 %collective-permute-start = (bf16[4,8,8,8,128]{4,2,1,3,0:T(8,128)(2,1)}, bf16[4,8,8,8,128]{4,2,1,3,0:T(8,128)(2,1)}, u32[]{:S(2)}, u32[]{:S(2)}) collective-permute-start(bf16[4,8,8,8,128]{4,2,1,3,0:T(8,128)(2,1)} %get-tuple-element.46), channel_id=1, source_target_pairs={{17,0},{18,1},{19,2},{20,3},{21,4},{22,5},{23,6},{24,7},{25,8},{26... | collective-permute-start | bytes 1572872 | tf_op jit(solution)/shard_map/ppermute | solution.py:14
  22.4 42.8 %collective-permute-start.1 = (bf16[4,8,8,8,128]{4,2,1,3,0:T(8,128)(2,1)}, bf16[4,8,8,8,128]{4,2,1,3,0:T(8,128)(2,1)}, u32[]{:S(2)}, u32[]{:S(2)}) collective-permute-start(bf16[4,8,8,8,128]{4,2,1,3,0:T(8,128)(2,1)} %get-tuple-element.45), channel_id=1, source_target_pairs={{16,0},{17,1},{18,2},{19,3},{20,4},{21,5},{22,6},{23,7},{24,8},{25... | collective-permute-start | bytes 1572872 | tf_op jit(solution)/shard_map/ppermute | solution.py:14
  25.7 47.9 %collective-permute-start.2 = (bf16[4,8,8,8,128]{4,2,1,3,0:T(8,128)(2,1)}, bf16[4,8,8,8,128]{4,2,1,3,0:T(8,128)(2,1)}, u32[]{:S(2)}, u32[]{:S(2)}) collective-permute-start(bf16[4,8,8,8,128]{4,2,1,3,0:T(8,128)(2,1)} %get-tuple-element.44), channel_id=1, source_target_pairs={{15,0},{16,1},{17,2},{18,3},{19,4},{20,5},{21,6},{22,7},{23,8},{24... | collective-permute-start | bytes 1572872 | tf_op jit(solution)/shard_map/ppermute | solution.py:14
  28.3 47.8 %collective-permute-start.3 = (bf16[4,8,8,8,128]{4,2,1,3,0:T(8,128)(2,1)}, bf16[4,8,8,8,128]{4,2,1,3,0:T(8,128)(2,1)}, u32[]{:S(2)}, u32[]{:S(2)}) collective-permute-start(bf16[4,8,8,8,128]{4,2,1,3,0:T(8,128)(2,1)} %get-tuple-element.43), channel_id=1, source_target_pairs={{1,0},{2,1},{3,2},{4,3},{5,4},{6,5},{7,6},{8,7},{9,8},{10,9},{11,1... | collective-permute-start | bytes 1572872 | tf_op jit(solution)/shard_map/ppermute | solution.py:14
  33.9 43.3 %collective-permute-start.4 = (bf16[4,8,8,8,128]{4,2,1,3,0:T(8,128)(2,1)}, bf16[4,8,8,8,128]{4,2,1,3,0:T(8,128)(2,1)}, u32[]{:S(2)}, u32[]{:S(2)}) collective-permute-start(bf16[4,8,8,8,128]{4,2,1,3,0:T(8,128)(2,1)} %get-tuple-element.42), channel_id=1, source_target_pairs={{0,1},{1,2},{2,3},{3,4},{4,5},{5,6},{6,7},{7,8},{8,9},{9,10},{10,1... | collective-permute-start | bytes 1572872 | tf_op jit(solution)/shard_map/ppermute | solution.py:14
  48.5 6.0 %copy-start.10 = (bf16[4,8,8,8,128]{4,2,1,3,0:T(8,128)(2,1)S(1)}, bf16[4,8,8,8,128]{4,2,1,3,0:T(8,128)(2,1)}, u32[]{:S(2)}) copy-start(bf16[4,8,8,8,128]{4,2,1,3,0:T(8,128)(2,1)} %get-tuple-element.41) | copy-start | bytes 1572868
  48.5 16.6 %copy-start.9 = (bf16[4,8,8,8,128]{4,2,1,3,0:T(8,128)(2,1)S(1)}, bf16[4,8,8,8,128]{4,2,1,3,0:T(8,128)(2,1)}, u32[]{:S(2)}) copy-start(bf16[4,8,8,8,128]{4,2,1,3,0:T(8,128)(2,1)} %get-tuple-element.40) | copy-start | bytes 1572868
  48.5 25.1 %copy-start.8 = (bf16[4,8,8,8,128]{4,2,1,3,0:T(8,128)(2,1)S(1)}, bf16[4,8,8,8,128]{4,2,1,3,0:T(8,128)(2,1)}, u32[]{:S(2)}) copy-start(bf16[4,8,8,8,128]{4,2,1,3,0:T(8,128)(2,1)} %get-tuple-element.39) | copy-start | bytes 1572868
  50.4 99.4 %copy-start.15 = (pred[16000]{0:T(1024)(128)(4,1)}, pred[16000]{0:T(1024)(128)(4,1)S(1)}, u32[]{:S(2)}) copy-start(pred[16000]{0:T(1024)(128)(4,1)S(1)} %compare_and_fusion) | copy-start | bytes 48004
  54.4 61.0 %copy-start.6 = (s32[16384]{0:T(1024)}, s32[16384]{0:T(1024)S(1)}, u32[]{:S(2)}) copy-start(s32[16384]{0:T(1024)S(1)} %pad_clamp_fusion) | copy-start | bytes 196612
  54.5 33.5 %copy-start.23 = (bf16[49]{0:T(256)(128)(2,1)}, bf16[49]{0:T(256)(128)(2,1)S(1)}, u32[]{:S(2)}) copy-start(bf16[49]{0:T(256)(128)(2,1)S(1)} %pad.11.clone) | copy-start | bytes 298
  54.5 23.8 %collective-permute-start.5 = (bf16[4,8,8,8,128]{4,2,1,3,0:T(8,128)(2,1)S(1)}, bf16[4,8,8,8,128]{4,2,1,3,0:T(8,128)(2,1)S(1)}, u32[]{:S(2)}, u32[]{:S(2)}) collective-permute-start(bf16[4,8,8,8,128]{4,2,1,3,0:T(8,128)(2,1)S(1)} %copy-done.10), channel_id=1, source_target_pairs={{0,15},{1,16},{2,17},{3,18},{4,19},{5,20},{6,21},{7,22},{8,23},{9,... | collective-permute-start | bytes 1572872 | tf_op jit(solution)/shard_map/ppermute | solution.py:14
  65.2 13.5 %collective-permute-start.6 = (bf16[4,8,8,8,128]{4,2,1,3,0:T(8,128)(2,1)S(1)}, bf16[4,8,8,8,128]{4,2,1,3,0:T(8,128)(2,1)S(1)}, u32[]{:S(2)}, u32[]{:S(2)}) collective-permute-start(bf16[4,8,8,8,128]{4,2,1,3,0:T(8,128)(2,1)S(1)} %copy-done.9), channel_id=1, source_target_pairs={{0,16},{1,17},{2,18},{3,19},{4,20},{5,21},{6,22},{7,23},{8,24},{9,... | collective-permute-start | bytes 1572872 | tf_op jit(solution)/shard_map/ppermute | solution.py:14
  73.7 10.6 %collective-permute-start.7 = (bf16[4,8,8,8,128]{4,2,1,3,0:T(8,128)(2,1)S(1)}, bf16[4,8,8,8,128]{4,2,1,3,0:T(8,128)(2,1)S(1)}, u32[]{:S(2)}, u32[]{:S(2)}) collective-permute-start(bf16[4,8,8,8,128]{4,2,1,3,0:T(8,128)(2,1)S(1)} %copy-done.8), channel_id=1, source_target_pairs={{0,17},{1,18},{2,19},{3,20},{4,21},{5,22},{6,23},{7,24},{8,25},{9,... | collective-permute-start | bytes 1572872 | tf_op jit(solution)/shard_map/ppermute | solution.py:14
  88.0 2.1 copy-start.2
  170.2 7.8 %copy-start.27 = (bf16[1,1,16,8,8,8,128]{6,5,4,3,2,1,0:T(8,128)(2,1)S(1)}, bf16[1,1,16,8,8,8,128]{6,5,4,3,2,1,0:T(8,128)(2,1)}, u32[]{:S(2)}) copy-start(bf16[1,1,16,8,8,8,128]{6,5,4,3,2,1,0:T(8,128)(2,1)} %param.19) | copy-start | bytes 6291460
  170.2 7.8 %copy-start.28 = (f32[128]{0:T(128)S(1)}, f32[128]{0:T(128)}, u32[]{:S(2)}) copy-start(f32[128]{0:T(128)} %param.21) | copy-start | bytes 1540
  196.6 23.3 %copy-start.3 = (bf16[16,8,8,8,128]{4,0,3,2,1:T(8,128)(2,1)}, bf16[16,8,8,8,128]{4,0,3,2,1:T(8,128)(2,1)S(1)}, u32[]{:S(2)}) copy-start(bf16[16,8,8,8,128]{4,0,3,2,1:T(8,128)(2,1)S(1)} %get-tuple-element.23) | copy-start | bytes 6291460
  220.7 1.2 copy-start.5
  221.9 5.2 %copy-start.1 = (bf16[16,8,8,8,128]{4,3,2,1,0:T(8,128)(2,1)S(1)}, bf16[16,8,8,8,128]{4,3,2,1,0:T(8,128)(2,1)}, u32[]{:S(2)}) copy-start(bf16[16,8,8,8,128]{4,3,2,1,0:T(8,128)(2,1)} %copy.175) | copy-start | bytes 6291460
  222.0 7.2 %copy-start.18 = (s32[1024]{0:T(1024)S(1)}, s32[1024]{0:T(1024)}, u32[]{:S(2)}) copy-start(s32[1024]{0:T(1024)} %copy-done.17) | copy-start | bytes 12292
  234.0 12.9 %copy-start.29 = (f32[128]{0:T(128)S(1)}, f32[128]{0:T(128)}, u32[]{:S(2)}) copy-start(f32[128]{0:T(128)} %get-tuple-element.22) | copy-start | bytes 1540
  238.4 106.0 %collective-permute-start.8 = (bf16[4,8,8,8,128]{4,3,2,1,0:T(8,128)(2,1)}, bf16[4,8,8,8,128]{4,3,2,1,0:T(8,128)(2,1)}, u32[]{:S(2)}, u32[]{:S(2)}) collective-permute-start(bf16[4,8,8,8,128]{4,3,2,1,0:T(8,128)(2,1)} %get-tuple-element.34), channel_id=1, source_target_pairs={{17,0},{18,1},{19,2},{20,3},{21,4},{22,5},{23,6},{24,7},{25,8},{26... | collective-permute-start | bytes 1572872 | tf_op jit(solution)/shard_map/ppermute | solution.py:14
  241.4 111.4 %collective-permute-start.9 = (bf16[4,8,8,8,128]{4,3,2,1,0:T(8,128)(2,1)}, bf16[4,8,8,8,128]{4,3,2,1,0:T(8,128)(2,1)}, u32[]{:S(2)}, u32[]{:S(2)}) collective-permute-start(bf16[4,8,8,8,128]{4,3,2,1,0:T(8,128)(2,1)} %get-tuple-element.33), channel_id=1, source_target_pairs={{16,0},{17,1},{18,2},{19,3},{20,4},{21,5},{22,6},{23,7},{24,8},{25... | collective-permute-start | bytes 1572872 | tf_op jit(solution)/shard_map/ppermute | solution.py:14
  245.0 110.9 %collective-permute-start.10 = (bf16[4,8,8,8,128]{4,3,2,1,0:T(8,128)(2,1)}, bf16[4,8,8,8,128]{4,3,2,1,0:T(8,128)(2,1)}, u32[]{:S(2)}, u32[]{:S(2)}) collective-permute-start(bf16[4,8,8,8,128]{4,3,2,1,0:T(8,128)(2,1)} %get-tuple-element.32), channel_id=1, source_target_pairs={{15,0},{16,1},{17,2},{18,3},{19,4},{20,5},{21,6},{22,7},{23,8},{24... | collective-permute-start | bytes 1572872 | tf_op jit(solution)/shard_map/ppermute | solution.py:14
  332.7 2.6 copy-start.14
  332.7 7.7 %copy-start.13 = (bf16[4,8,8,8,128]{4,3,2,1,0:T(8,128)(2,1)S(1)}, bf16[4,8,8,8,128]{4,3,2,1,0:T(8,128)(2,1)}, u32[]{:S(2)}) copy-start(bf16[4,8,8,8,128]{4,3,2,1,0:T(8,128)(2,1)} %get-tuple-element.30) | copy-start | bytes 1572868
  332.7 9.8 %copy-start.4 = (bf16[1,1,16,8,8,8,128]{6,2,5,4,3,1,0:T(8,128)(2,1)S(1)}, bf16[1,1,16,8,8,8,128]{6,2,5,4,3,1,0:T(8,128)(2,1)}, u32[]{:S(2)}) copy-start(bf16[1,1,16,8,8,8,128]{6,2,5,4,3,1,0:T(8,128)(2,1)} %get-tuple-element.24) | copy-start | bytes 6291460
  333.2 11.2 %copy-start.12 = (bf16[4,8,8,8,128]{4,3,2,1,0:T(8,128)(2,1)S(1)}, bf16[4,8,8,8,128]{4,3,2,1,0:T(8,128)(2,1)}, u32[]{:S(2)}) copy-start(bf16[4,8,8,8,128]{4,3,2,1,0:T(8,128)(2,1)} %get-tuple-element.29) | copy-start | bytes 1572868
  335.3 17.5 %copy-start.11 = (bf16[4,8,8,8,128]{4,3,2,1,0:T(8,128)(2,1)S(1)}, bf16[4,8,8,8,128]{4,3,2,1,0:T(8,128)(2,1)}, u32[]{:S(2)}) copy-start(bf16[4,8,8,8,128]{4,3,2,1,0:T(8,128)(2,1)} %get-tuple-element.28) | copy-start | bytes 1572868
  335.3 23.0 %collective-permute-start.11 = (bf16[4,8,8,8,128]{4,3,2,1,0:T(8,128)(2,1)S(1)}, bf16[4,8,8,8,128]{4,3,2,1,0:T(8,128)(2,1)S(1)}, u32[]{:S(2)}, u32[]{:S(2)}) collective-permute-start(bf16[4,8,8,8,128]{4,3,2,1,0:T(8,128)(2,1)S(1)} %copy-done.14), channel_id=1, source_target_pairs={{1,0},{2,1},{3,2},{4,3},{5,4},{6,5},{7,6},{8,7},{9,8},{10,9},{11,1... | collective-permute-start | bytes 1572872 | tf_op jit(solution)/shard_map/ppermute | solution.py:14
  340.4 20.0 %collective-permute-start.12 = (bf16[4,8,8,8,128]{4,3,2,1,0:T(8,128)(2,1)S(1)}, bf16[4,8,8,8,128]{4,3,2,1,0:T(8,128)(2,1)S(1)}, u32[]{:S(2)}, u32[]{:S(2)}) collective-permute-start(bf16[4,8,8,8,128]{4,3,2,1,0:T(8,128)(2,1)S(1)} %copy-done.13), channel_id=1, source_target_pairs={{0,1},{1,2},{2,3},{3,4},{4,5},{5,6},{6,7},{7,8},{8,9},{9,10},{10,1... | collective-permute-start | bytes 1572872 | tf_op jit(solution)/shard_map/ppermute | solution.py:14
  344.4 19.0 %collective-permute-start.13 = (bf16[4,8,8,8,128]{4,3,2,1,0:T(8,128)(2,1)S(1)}, bf16[4,8,8,8,128]{4,3,2,1,0:T(8,128)(2,1)S(1)}, u32[]{:S(2)}, u32[]{:S(2)}) collective-permute-start(bf16[4,8,8,8,128]{4,3,2,1,0:T(8,128)(2,1)S(1)} %copy-done.12), channel_id=1, source_target_pairs={{0,15},{1,16},{2,17},{3,18},{4,19},{5,20},{6,21},{7,22},{8,23},{9,... | collective-permute-start | bytes 1572872 | tf_op jit(solution)/shard_map/ppermute | solution.py:14
  352.8 24.4 %collective-permute-start.14 = (bf16[4,8,8,8,128]{4,3,2,1,0:T(8,128)(2,1)S(1)}, bf16[4,8,8,8,128]{4,3,2,1,0:T(8,128)(2,1)S(1)}, u32[]{:S(2)}, u32[]{:S(2)}) collective-permute-start(bf16[4,8,8,8,128]{4,3,2,1,0:T(8,128)(2,1)S(1)} %copy-done.11), channel_id=1, source_target_pairs={{0,16},{1,17},{2,18},{3,19},{4,20},{5,21},{6,22},{7,23},{8,24},{9,... | collective-permute-start | bytes 1572872 | tf_op jit(solution)/shard_map/ppermute | solution.py:14
  355.9 21.4 %collective-permute-start.15 = (bf16[4,8,8,8,128]{4,3,2,1,0:T(8,128)(2,1)S(1)}, bf16[4,8,8,8,128]{4,3,2,1,0:T(8,128)(2,1)S(1)}, u32[]{:S(2)}, u32[]{:S(2)}) collective-permute-start(bf16[4,8,8,8,128]{4,3,2,1,0:T(8,128)(2,1)S(1)} %get-tuple-element.27), channel_id=1, source_target_pairs={{0,17},{1,18},{2,19},{3,20},{4,21},{5,22},{6,23},{7,24},{8,25},{9,... | collective-permute-start | bytes 1572872 | tf_op jit(solution)/shard_map/ppermute | solution.py:14
  379.7 0.7 copy-start.24
  380.9 25.4 %copy-start.7 = (s32[16384]{0:T(1024)S(1)}, s32[16384]{0:T(1024)}, u32[]{:S(2)}) copy-start(s32[16384]{0:T(1024)} %copy-done.6) | copy-start | bytes 196612
  406.2 34.3 %copy-start.16 = (pred[16000]{0:T(1024)(128)(4,1)S(1)}, pred[16000]{0:T(1024)(128)(4,1)}, u32[]{:S(2)}) copy-start(pred[16000]{0:T(1024)(128)(4,1)} %copy-done.15) | copy-start | bytes 48004
Sparse Core Ops, SparseCore 0:
  222.1 181.5 all-reduce.3
where the time goes:
time: 498 us; the launch traced here: 490 us
  local copies, waits for them, and re-layouts  167 us (34%)
  blocking collectives  85.8 us (17%)
  other arithmetic  84.6 us (17%)
  matrix products  57.6 us (12%)
  starting transfers between devices  55.9 us (11%)
  waiting for transfers between devices  24.5 us (5%)
  between operations  15.1 us (3%)
    psum x1, blocking collectives, shards(): weight_total, bias_total = lax.psum((weight_part, bias_part), ('gx', 'gy'))  85.8 us
    gather x2, local copies, waits for them, and re-layouts, assemble(): gathered = jnp.take(pool, row_ids.reshape(-1), axis=0)  68.6 us
    ppermute x16, starting transfers between devices, passed_along(): return lax.ppermute(block, axis, route)  55.8 us
    concatenate x2, other arithmetic, assemble(): jnp.concatenate([volume.reshape(-1, channels), face_table.reshape(-1, cha...  50.6 us
    conv_general_dilated x2, matrix products, conv_valid(): lax.conv_general_dilated(padded, kernel, (1, 1, 1), 'VALID', dimension_nu...  36.2 us
    unnamed x98, local copies, waits for them, and re-layouts  29.6 us
    reshape x3, local copies, waits for them, and re-layouts, assemble(): return gathered.reshape(brick_count, side, side, side, channels)  24.7 us
    select_n x3, other arithmetic, assemble(): gathered = jnp.take(pool, row_ids.reshape(-1), axis=0)  24.6 us
  transfers between devices with their start and end apart: 17, of which 5 were waited for; matrix products, arithmetic and copies ran while one was open for 32% of the time, Pallas kernels for 0%

commit v1 on v0

--- a/solution.py
+++ b/solution.py
@@ -157,7 +157,7 @@
     input_grad = conv_valid(grad_padded, flipped).astype(jnp.bfloat16)
     weight_part = weight_terms(padded, slope_grad)
     bias_part = jnp.sum(slope_grad, axis=(0, 1, 2, 3), dtype=jnp.float32)
-    weight_total, bias_total = lax.psum((weight_part, bias_part), ("gx", "gy"))
+    weight_total, bias_total = lax.psum(lax.psum((weight_part, bias_part), "gx"), "gy")
     edge_len = volume.shape[1]
     total_voxels = (
         lax.axis_size("gx") * lax.axis_size("gy") * volume.shape[0] * edge_len * edge_len * edge_len

time: 498 us -> 531 us (1.066)
  waiting for transfers between devices: 24.5 us -> 69 us
  blocking collectives: 85.8 us -> 67.7 us
  starting transfers between devices: 55.9 us -> 62.2 us
    psum x1 -> x2, waiting for transfers between devices: 0.01 us -> 45.2 us  [the longest x1 45.2 us: shards(): lax.psum(lax.psum((weight_part, bias_part), 'gx'), 'gy')]
    psum x1 -> x2, blocking collectives: 85.8 us -> 67.7 us  [the longest x1 42.5 us: shards(): lax.psum(lax.psum((weight_part, bias_part), 'gx'), 'gy')]
    ppermute x16, starting transfers between devices: 55.8 us -> 62.1 us  [passed_along(): return lax.ppermute(block, axis, route)]
  transfers between devices with their start and end apart: 17 -> 18, of which waited for: 5 -> 5; matrix products, arithmetic and copies ran while one was open for 32% -> 30% of each run, Pallas kernels for 0% -> 0%
where the time goes in v1:
time: 531 us; the launch traced here: 523 us
  local copies, waits for them, and re-layouts  166 us (31%)
  other arithmetic  84.6 us (16%)
  waiting for transfers between devices  69 us (13%)
  blocking collectives  67.7 us (13%)
  starting transfers between devices  62.2 us (12%)
  matrix products  57.6 us (11%)
  between operations  15.4 us (3%)
    gather x2, local copies, waits for them, and re-layouts, assemble(): gathered = jnp.take(pool, row_ids.reshape(-1), axis=0)  68.5 us
    ppermute x16, starting transfers between devices, passed_along(): return lax.ppermute(block, axis, route)  62.1 us
    concatenate x2, other arithmetic, assemble(): jnp.concatenate([volume.reshape(-1, channels), face_table.reshape(-1, cha...  50.6 us
    psum x1, waiting for transfers between devices, shards(): lax.psum(lax.psum((weight_part, bias_part), 'gx'), 'gy')  45.2 us
    psum x1, blocking collectives, shards(): lax.psum(lax.psum((weight_part, bias_part), 'gx'), 'gy')  42.5 us
    conv_general_dilated x2, matrix products, conv_valid(): lax.conv_general_dilated(padded, kernel, (1, 1, 1), 'VALID', dimension_nu...  36.5 us
    unnamed x98, local copies, waits for them, and re-layouts  29.6 us
    psum x1, blocking collectives, shards(): lax.psum((weight_part, bias_part), 'gx')  25.2 us
  transfers between devices with their start and end apart: 18, of which 5 were waited for; matrix products, arithmetic and copies ran while one was open for 30% of the time, Pallas kernels for 0%

profile of v1, /device:TPU:1, one launch (start us, length us, event | category | flops | bytes accessed | tf_op | source)
XLA Modules:
  0.0 522.8 jit_solution(13497586762802757675)
XLA Ops:
  7.2 2.2 copy.277
  9.6 2.0 concatenate.18
  11.7 4.7 gather_fusion
  16.4 4.5 fusion.54
  22.3 3.3 collective-permute-start.1
  25.7 2.6 collective-permute-start.2
  28.2 5.6 %collective-permute-start.3 = (bf16[4,8,8,8,128]{4,2,1,3,0:T(8,128)(2,1)}, bf16[4,8,8,8,128]{4,2,1,3,0:T(8,128)(2,1)}, u32[]{:S(2)}, u32[]{:S(2)}) collective-permute-start(bf16[4,8,8,8,128]{4,2,1,3,0:T(8,128)(2,1)} %get-tuple-element.43), channel_id=1, source_target_pairs={{1,0},{2,1},{3,2},{4,3},{5,4},{6,5},{7,6},{8,7},{9,8},{10,9},{11,1... | collective-permute-start | bytes 1572872 | tf_op jit(solution)/shard_map/ppermute | solution.py:14
  33.8 1.9 collective-permute-start.4
  38.6 4.0 gather_fusion.2
  42.6 2.5 fusion.42
  45.1 1.8 copy.159
  54.5 9.5 %collective-permute-start.5 = (bf16[4,8,8,8,128]{4,2,1,3,0:T(8,128)(2,1)S(1)}, bf16[4,8,8,8,128]{4,2,1,3,0:T(8,128)(2,1)S(1)}, u32[]{:S(2)}, u32[]{:S(2)}) collective-permute-start(bf16[4,8,8,8,128]{4,2,1,3,0:T(8,128)(2,1)S(1)} %copy-done.10), channel_id=1, source_target_pairs={{0,15},{1,16},{2,17},{3,18},{4,19},{5,20},{6,21},{7,22},{8,23},{9,... | collective-permute-start | bytes 1572872 | tf_op jit(solution)/shard_map/ppermute | solution.py:14
  65.1 7.3 %collective-permute-start.6 = (bf16[4,8,8,8,128]{4,2,1,3,0:T(8,128)(2,1)S(1)}, bf16[4,8,8,8,128]{4,2,1,3,0:T(8,128)(2,1)S(1)}, u32[]{:S(2)}, u32[]{:S(2)}) collective-permute-start(bf16[4,8,8,8,128]{4,2,1,3,0:T(8,128)(2,1)S(1)} %copy-done.9), channel_id=1, source_target_pairs={{0,16},{1,17},{2,18},{3,19},{4,20},{5,21},{6,22},{7,23},{8,24},{9,... | collective-permute-start | bytes 1572872 | tf_op jit(solution)/shard_map/ppermute | solution.py:14
  78.6 5.6 %collective-permute-done.7 = bf16[4,8,8,8,128]{4,2,1,3,0:T(8,128)(2,1)S(1)} collective-permute-done((bf16[4,8,8,8,128]{4,2,1,3,0:T(8,128)(2,1)S(1)}, bf16[4,8,8,8,128]{4,2,1,3,0:T(8,128)(2,1)S(1)}, u32[]{:S(2)}, u32[]{:S(2)}) %collective-permute-start.7) | collective-permute-done | bytes 524320 | tf_op jit(solution)/shard_map/ppermute | solution.py:14
  84.6 2.7 fusion.52
  88.2 2.1 maximum_maximum_fusion
  90.4 25.3 %pad_maximum_fusion = bf16[27008,128]{1,0:T(8,128)(2,1)} fusion(bf16[18816,128]{1,0:T(8,128)(2,1)S(1)} %bitcast.412, bf16[8192,128]{1,0:T(8,128)(2,1)S(1)} %bitcast.420), kind=kLoop, calls=%fused_computation.5 | loop fusion | flops 13828096 | bytes 13828096 | tf_op jit(solution)/shard_map/concatenate | solution.py:90
  115.7 34.3 %gather_fusion.3 = bf16[16000,128]{1,0:T(8,128)(2,1)} fusion(bf16[27008,128]{1,0:T(8,128)(2,1)} %pad_maximum_fusion, s32[16384]{0:T(1024)S(1)} %pad_clamp_fusion), kind=kCustom, calls=%fused_computation.1.clone | custom fusion | bytes 8256000 | tf_op jit(solution)/shard_map/jit(_take)/gather | solution.py:91
  150.0 11.8 %broadcast_select_fusion.1 = bf16[16000,128]{1,0:T(8,128)(2,1)} fusion(bf16[16000,128]{1,0:T(8,128)(2,1)} %gather_fusion.3, pred[16000]{0:T(1024)(128)(4,1)S(1)} %compare_and_fusion), kind=kLoop, calls=%fused_computation.18 | loop fusion | flops 2048000 | bytes 8208000 | tf_op jit(solution)/shard_map/jit(_take)/select_n | solution.py:91
  161.8 8.4 %reshape.121 = bf16[16,10,10,10,128]{4,3,2,1,0:T(8,128)(2,1)} reshape(bf16[16000,128]{1,0:T(8,128)(2,1)} %broadcast_select_fusion.1) | data formatting | bytes 8192000 | tf_op jit(solution)/shard_map/reshape | solution.py:92
  170.2 7.7 %copy.173 = bf16[16,10,10,10,128]{4,0,3,2,1:T(8,128)(2,1)S(1)} copy(bf16[16,10,10,10,128]{4,3,2,1,0:T(8,128)(2,1)} %reshape.121) | data formatting | bytes 8192000 | tf_op jit(solution)/shard_map/reshape | solution.py:92
  178.0 18.8 %convert_reduce_fusion = (f32[128]{0:T(128)}, bf16[16,8,8,8,128]{4,0,3,2,1:T(8,128)(2,1)S(1)}, bf16[1,1,16,8,8,8,128]{6,2,5,4,3,1,0:T(8,128)(2,1)}) fusion(f32[128]{0:T(128)S(1)} %copy-done.28, bf16[1,1,16,8,8,8,128]{6,5,4,3,2,1,0:T(8,128)(2,1)S(1)} %copy-done.27, bf16[16,10,10,10,128]{4,0,3,2,1:T(8,128)(2,1)S(1)} %copy.173, ...), kind=kOutput, calls=%fused_computation.12 | convolution fusion | flops 7263485952 | bytes 11273216 | tf_op jit(solution)/shard_map/conv_general_dilated | solution.py:96
  198.4 1.9 copy.175
  222.0 1.8 slice_dynamic-update-slice_fusion.2
  227.1 2.1 concatenate.21.clone
  229.2 4.7 gather_fusion.1
  233.9 4.4 fusion.51
  241.2 1.9 collective-permute-start.9
  244.8 1.9 collective-permute-start.10
  246.7 25.2 %psum.30 = f32[128]{0:T(128)S(1)} all-reduce(f32[128]{0:T(128)S(1)} %copy-done.29), channel_id=1, replica_groups=mesh['gx'=8,'gy'=16] {'gx'}, use_global_device_ids=true, to_apply=%region_3.6 | all-reduce | flops 128 | bytes 1024 | tf_op jit(solution)/shard_map/psum | solution.py:160
  271.9 42.5 %psum.31 = f32[128]{0:T(128)S(1)} all-reduce(f32[128]{0:T(128)S(1)} %psum.30), channel_id=1, replica_groups=mesh['gx'=8,'gy'=16] {'gy'}, use_global_device_ids=true, to_apply=%region_4.7 | all-reduce | flops 128 | bytes 1024 | tf_op jit(solution)/shard_map/psum | solution.py:160
  314.9 2.1 copy.184
  317.0 10.3 %collective-permute-start.11 = (bf16[4,8,8,8,128]{4,3,2,1,0:T(8,128)(2,1)S(1)}, bf16[4,8,8,8,128]{4,3,2,1,0:T(8,128)(2,1)S(1)}, u32[]{:S(2)}, u32[]{:S(2)}) collective-permute-start(bf16[4,8,8,8,128]{4,3,2,1,0:T(8,128)(2,1)S(1)} %copy-done.14), channel_id=1, source_target_pairs={{1,0},{2,1},{3,2},{4,3},{5,4},{6,5},{7,6},{8,7},{9,8},{10,9},{11,1... | collective-permute-start | bytes 1572872 | tf_op jit(solution)/shard_map/ppermute | solution.py:14
  327.3 1.9 collective-permute-start.12
  329.2 1.9 copy.213
  331.1 7.7 %collective-permute-start.13 = (bf16[4,8,8,8,128]{4,3,2,1,0:T(8,128)(2,1)S(1)}, bf16[4,8,8,8,128]{4,3,2,1,0:T(8,128)(2,1)S(1)}, u32[]{:S(2)}, u32[]{:S(2)}) collective-permute-start(bf16[4,8,8,8,128]{4,3,2,1,0:T(8,128)(2,1)S(1)} %copy-done.12), channel_id=1, source_target_pairs={{0,15},{1,16},{2,17},{3,18},{4,19},{5,20},{6,21},{7,22},{8,23},{9,... | collective-permute-start | bytes 1572872 | tf_op jit(solution)/shard_map/ppermute | solution.py:14
  339.9 2.4 collective-permute-start.14
  346.5 3.9 collective-permute-done.13
  350.5 14.1 %collective-permute-done.14 = bf16[4,8,8,8,128]{4,3,2,1,0:T(8,128)(2,1)S(1)} collective-permute-done((bf16[4,8,8,8,128]{4,3,2,1,0:T(8,128)(2,1)S(1)}, bf16[4,8,8,8,128]{4,3,2,1,0:T(8,128)(2,1)S(1)}, u32[]{:S(2)}, u32[]{:S(2)}) %collective-permute-start.14) | collective-permute-done | bytes 524320 | tf_op jit(solution)/shard_map/ppermute | solution.py:14
  364.8 2.2 fusion.50
  368.2 25.3 %pad_maximum_fusion.1 = bf16[27008,128]{1,0:T(8,128)(2,1)} fusion(bf16[18816,128]{1,0:T(8,128)(2,1)S(1)} %bitcast.411, bf16[8192,128]{1,0:T(8,128)(2,1)S(1)} %bitcast.418), kind=kLoop, calls=%fused_computation.6 | loop fusion | flops 13828096 | bytes 13828096 | tf_op jit(solution)/shard_map/concatenate | solution.py:90
  393.5 34.3 %gather_fusion.4 = bf16[16000,128]{1,0:T(8,128)(2,1)} fusion(bf16[27008,128]{1,0:T(8,128)(2,1)} %pad_maximum_fusion.1, s32[16384]{0:T(1024)S(1)} %copy-done.7), kind=kCustom, calls=%fused_computation.2.clone | custom fusion | bytes 8256000 | tf_op jit(solution)/shard_map/jit(_take)/gather | solution.py:91
  427.8 11.9 %broadcast_select_fusion = bf16[16000,128]{1,0:T(8,128)(2,1)} fusion(bf16[16000,128]{1,0:T(8,128)(2,1)} %gather_fusion.4, pred[16000]{0:T(1024)(128)(4,1)S(1)} %copy-done.16), kind=kLoop, calls=%fused_computation.17 | loop fusion | flops 2048000 | bytes 8208000 | tf_op jit(solution)/shard_map/jit(_take)/select_n | solution.py:91
  439.7 8.3 %reshape.126 = bf16[16,10,10,10,128]{4,3,2,1,0:T(8,128)(2,1)} reshape(bf16[16000,128]{1,0:T(8,128)(2,1)} %broadcast_select_fusion) | data formatting | bytes 8192000 | tf_op jit(solution)/shard_map/reshape | solution.py:92
  448.0 17.6 %convert_bitcast_fusion = bf16[1,1,16,8,8,8,128]{6,2,5,4,3,1,0:T(8,128)(2,1)S(1)} fusion(bf16[3,3,3,128,128]{4,3,2,1,0:T(8,128)(2,1)S(1)} %copy-done, bf16[16,10,10,10,128]{4,3,2,1,0:T(8,128)(2,1)} %reshape.126), kind=kOutput, calls=%fused_computation.20 | convolution fusion | flops 7248805888 | bytes 7077888 | tf_op jit(solution)/shard_map/conv_general_dilated | solution.py:96
  465.6 1.9 copy.214
  467.5 45.2 %all-reduce.7.cloned.1.call-done = f32[3,3,3,128,128]{4,3,2,1,0:T(8,128)} async-done(((f32[3,3,3,128,128]{4,3,2,1,0:T(8,128)}), f32[3,3,3,128,128]{4,3,2,1,0:T(8,128)}) %all-reduce.7.cloned.1.call-update) | async-done | bytes 1769488 | tf_op jit(solution)/shard_map/psum | solution.py:160
  512.7 2.9 broadcast_multiply_fusion
  (164 shorter events, 58.7 us)
Async XLA Ops:
  7.2 170.8 %copy-start = (bf16[3,3,3,128,128]{4,3,2,1,0:T(8,128)(2,1)S(1)}, bf16[3,3,3,128,128]{4,3,2,1,0:T(8,128)(2,1)}, u32[]{:S(2)}) copy-start(bf16[3,3,3,128,128]{4,3,2,1,0:T(8,128)(2,1)} %param.20) | copy-start | bytes 2654212
  7.2 2.3 copy-start.25
  7.2 420.6 %all-reduce.5.cloned.1.call-start = ((), (), s32[]{:S(2)}) async-start(), calls=%async_computation | async-start | bytes 3538944 | tf_op jit(solution)/shard_map/psum | solution.py:160
  9.5 2.2 copy-start.22
  11.7 4.7 copy-start.17
  20.9 17.6 %copy-start.19 = (s32[1,1,16,27]{3,2,1,0:T(8,128)S(1)}, s32[1,1,16,27]{3,2,1,0:T(8,128)}, u32[]{:S(2)}) copy-start(s32[1,1,16,27]{3,2,1,0:T(8,128)} %param.23) | copy-start | bytes 5188
  20.9 21.7 %copy-start.20 = (s32[1000]{0:T(1024)S(1)}, s32[1000]{0:T(1024)}, u32[]{:S(2)}) copy-start(s32[1000]{0:T(1024)} %constant.18.clone) | copy-start | bytes 12004
  20.9 21.7 %copy-start.21 = (s32[1000]{0:T(1024)S(1)}, s32[1000]{0:T(1024)}, u32[]{:S(2)}) copy-start(s32[1000]{0:T(1024)} %constant.19.clone) | copy-start | bytes 12004
  20.9 21.7 %copy-start.26 = (pred[1000]{0:T(1024)(128)(4,1)S(1)}, pred[1000]{0:T(1024)(128)(4,1)}, u32[]{:S(2)}) copy-start(pred[1000]{0:T(1024)(128)(4,1)} %constant.20.clone) | copy-start | bytes 3004
  20.9 33.6 %collective-permute-start = (bf16[4,8,8,8,128]{4,2,1,3,0:T(8,128)(2,1)}, bf16[4,8,8,8,128]{4,2,1,3,0:T(8,128)(2,1)}, u32[]{:S(2)}, u32[]{:S(2)}) collective-permute-start(bf16[4,8,8,8,128]{4,2,1,3,0:T(8,128)(2,1)} %get-tuple-element.46), channel_id=1, source_target_pairs={{17,0},{18,1},{19,2},{20,3},{21,4},{22,5},{23,6},{24,7},{25,8},{26... | collective-permute-start | bytes 1572872 | tf_op jit(solution)/shard_map/ppermute | solution.py:14
  22.3 42.8 %collective-permute-start.1 = (bf16[4,8,8,8,128]{4,2,1,3,0:T(8,128)(2,1)}, bf16[4,8,8,8,128]{4,2,1,3,0:T(8,128)(2,1)}, u32[]{:S(2)}, u32[]{:S(2)}) collective-permute-start(bf16[4,8,8,8,128]{4,2,1,3,0:T(8,128)(2,1)} %get-tuple-element.45), channel_id=1, source_target_pairs={{16,0},{17,1},{18,2},{19,3},{20,4},{21,5},{22,6},{23,7},{24,8},{25... | collective-permute-start | bytes 1572872 | tf_op jit(solution)/shard_map/ppermute | solution.py:14
  25.7 47.9 %collective-permute-start.2 = (bf16[4,8,8,8,128]{4,2,1,3,0:T(8,128)(2,1)}, bf16[4,8,8,8,128]{4,2,1,3,0:T(8,128)(2,1)}, u32[]{:S(2)}, u32[]{:S(2)}) collective-permute-start(bf16[4,8,8,8,128]{4,2,1,3,0:T(8,128)(2,1)} %get-tuple-element.44), channel_id=1, source_target_pairs={{15,0},{16,1},{17,2},{18,3},{19,4},{20,5},{21,6},{22,7},{23,8},{24... | collective-permute-start | bytes 1572872 | tf_op jit(solution)/shard_map/ppermute | solution.py:14
  28.2 47.8 %collective-permute-start.3 = (bf16[4,8,8,8,128]{4,2,1,3,0:T(8,128)(2,1)}, bf16[4,8,8,8,128]{4,2,1,3,0:T(8,128)(2,1)}, u32[]{:S(2)}, u32[]{:S(2)}) collective-permute-start(bf16[4,8,8,8,128]{4,2,1,3,0:T(8,128)(2,1)} %get-tuple-element.43), channel_id=1, source_target_pairs={{1,0},{2,1},{3,2},{4,3},{5,4},{6,5},{7,6},{8,7},{9,8},{10,9},{11,1... | collective-permute-start | bytes 1572872 | tf_op jit(solution)/shard_map/ppermute | solution.py:14
  33.8 43.3 %collective-permute-start.4 = (bf16[4,8,8,8,128]{4,2,1,3,0:T(8,128)(2,1)}, bf16[4,8,8,8,128]{4,2,1,3,0:T(8,128)(2,1)}, u32[]{:S(2)}, u32[]{:S(2)}) collective-permute-start(bf16[4,8,8,8,128]{4,2,1,3,0:T(8,128)(2,1)} %get-tuple-element.42), channel_id=1, source_target_pairs={{0,1},{1,2},{2,3},{3,4},{4,5},{5,6},{6,7},{7,8},{8,9},{9,10},{10,1... | collective-permute-start | bytes 1572872 | tf_op jit(solution)/shard_map/ppermute | solution.py:14
  48.5 6.0 %copy-start.10 = (bf16[4,8,8,8,128]{4,2,1,3,0:T(8,128)(2,1)S(1)}, bf16[4,8,8,8,128]{4,2,1,3,0:T(8,128)(2,1)}, u32[]{:S(2)}) copy-start(bf16[4,8,8,8,128]{4,2,1,3,0:T(8,128)(2,1)} %get-tuple-element.41) | copy-start | bytes 1572868
  48.5 16.6 %copy-start.9 = (bf16[4,8,8,8,128]{4,2,1,3,0:T(8,128)(2,1)S(1)}, bf16[4,8,8,8,128]{4,2,1,3,0:T(8,128)(2,1)}, u32[]{:S(2)}) copy-start(bf16[4,8,8,8,128]{4,2,1,3,0:T(8,128)(2,1)} %get-tuple-element.40) | copy-start | bytes 1572868
  48.5 25.1 %copy-start.8 = (bf16[4,8,8,8,128]{4,2,1,3,0:T(8,128)(2,1)S(1)}, bf16[4,8,8,8,128]{4,2,1,3,0:T(8,128)(2,1)}, u32[]{:S(2)}) copy-start(bf16[4,8,8,8,128]{4,2,1,3,0:T(8,128)(2,1)} %get-tuple-element.39) | copy-start | bytes 1572868
  50.3 99.7 %copy-start.15 = (pred[16000]{0:T(1024)(128)(4,1)}, pred[16000]{0:T(1024)(128)(4,1)S(1)}, u32[]{:S(2)}) copy-start(pred[16000]{0:T(1024)(128)(4,1)S(1)} %compare_and_fusion) | copy-start | bytes 48004
  54.4 61.3 %copy-start.6 = (s32[16384]{0:T(1024)}, s32[16384]{0:T(1024)S(1)}, u32[]{:S(2)}) copy-start(s32[16384]{0:T(1024)S(1)} %pad_clamp_fusion) | copy-start | bytes 196612
  54.5 33.8 %copy-start.23 = (bf16[49]{0:T(256)(128)(2,1)}, bf16[49]{0:T(256)(128)(2,1)S(1)}, u32[]{:S(2)}) copy-start(bf16[49]{0:T(256)(128)(2,1)S(1)} %pad.11.clone) | copy-start | bytes 298
  54.5 23.8 %collective-permute-start.5 = (bf16[4,8,8,8,128]{4,2,1,3,0:T(8,128)(2,1)S(1)}, bf16[4,8,8,8,128]{4,2,1,3,0:T(8,128)(2,1)S(1)}, u32[]{:S(2)}, u32[]{:S(2)}) collective-permute-start(bf16[4,8,8,8,128]{4,2,1,3,0:T(8,128)(2,1)S(1)} %copy-done.10), channel_id=1, source_target_pairs={{0,15},{1,16},{2,17},{3,18},{4,19},{5,20},{6,21},{7,22},{8,23},{9,... | collective-permute-start | bytes 1572872 | tf_op jit(solution)/shard_map/ppermute | solution.py:14
  65.1 13.5 %collective-permute-start.6 = (bf16[4,8,8,8,128]{4,2,1,3,0:T(8,128)(2,1)S(1)}, bf16[4,8,8,8,128]{4,2,1,3,0:T(8,128)(2,1)S(1)}, u32[]{:S(2)}, u32[]{:S(2)}) collective-permute-start(bf16[4,8,8,8,128]{4,2,1,3,0:T(8,128)(2,1)S(1)} %copy-done.9), channel_id=1, source_target_pairs={{0,16},{1,17},{2,18},{3,19},{4,20},{5,21},{6,22},{7,23},{8,24},{9,... | collective-permute-start | bytes 1572872 | tf_op jit(solution)/shard_map/ppermute | solution.py:14
  73.6 10.6 %collective-permute-start.7 = (bf16[4,8,8,8,128]{4,2,1,3,0:T(8,128)(2,1)S(1)}, bf16[4,8,8,8,128]{4,2,1,3,0:T(8,128)(2,1)S(1)}, u32[]{:S(2)}, u32[]{:S(2)}) collective-permute-start(bf16[4,8,8,8,128]{4,2,1,3,0:T(8,128)(2,1)S(1)} %copy-done.8), channel_id=1, source_target_pairs={{0,17},{1,18},{2,19},{3,20},{4,21},{5,22},{6,23},{7,24},{8,25},{9,... | collective-permute-start | bytes 1572872 | tf_op jit(solution)/shard_map/ppermute | solution.py:14
  88.2 2.1 copy-start.2
  170.2 7.8 %copy-start.27 = (bf16[1,1,16,8,8,8,128]{6,5,4,3,2,1,0:T(8,128)(2,1)S(1)}, bf16[1,1,16,8,8,8,128]{6,5,4,3,2,1,0:T(8,128)(2,1)}, u32[]{:S(2)}) copy-start(bf16[1,1,16,8,8,8,128]{6,5,4,3,2,1,0:T(8,128)(2,1)} %param.19) | copy-start | bytes 6291460
  170.2 7.8 %copy-start.28 = (f32[128]{0:T(128)S(1)}, f32[128]{0:T(128)}, u32[]{:S(2)}) copy-start(f32[128]{0:T(128)} %param.21) | copy-start | bytes 1540
  196.8 23.1 %copy-start.3 = (bf16[16,8,8,8,128]{4,0,3,2,1:T(8,128)(2,1)}, bf16[16,8,8,8,128]{4,0,3,2,1:T(8,128)(2,1)S(1)}, u32[]{:S(2)}) copy-start(bf16[16,8,8,8,128]{4,0,3,2,1:T(8,128)(2,1)S(1)} %get-tuple-element.23) | copy-start | bytes 6291460
  220.7 1.2 copy-start.5
  221.9 5.2 copy-start.1
  222.0 7.2 %copy-start.18 = (s32[1024]{0:T(1024)S(1)}, s32[1024]{0:T(1024)}, u32[]{:S(2)}) copy-start(s32[1024]{0:T(1024)} %copy-done.17) | copy-start | bytes 12292
  222.0 290.7 %all-reduce.7.cloned.1.call-start = ((), (), s32[]{:S(2)}) async-start(), calls=%async_computation.1 | async-start | bytes 3538944 | tf_op jit(solution)/shard_map/psum | solution.py:160
  233.9 12.9 %copy-start.29 = (f32[128]{0:T(128)S(1)}, f32[128]{0:T(128)}, u32[]{:S(2)}) copy-start(f32[128]{0:T(128)} %get-tuple-element.22) | copy-start | bytes 1540
  238.2 92.9 %collective-permute-start.8 = (bf16[4,8,8,8,128]{4,3,2,1,0:T(8,128)(2,1)}, bf16[4,8,8,8,128]{4,3,2,1,0:T(8,128)(2,1)}, u32[]{:S(2)}, u32[]{:S(2)}) collective-permute-start(bf16[4,8,8,8,128]{4,3,2,1,0:T(8,128)(2,1)} %get-tuple-element.34), channel_id=1, source_target_pairs={{17,0},{18,1},{19,2},{20,3},{21,4},{22,5},{23,6},{24,7},{25,8},{26... | collective-permute-start | bytes 1572872 | tf_op jit(solution)/shard_map/ppermute | solution.py:14
  241.2 98.7 %collective-permute-start.9 = (bf16[4,8,8,8,128]{4,3,2,1,0:T(8,128)(2,1)}, bf16[4,8,8,8,128]{4,3,2,1,0:T(8,128)(2,1)}, u32[]{:S(2)}, u32[]{:S(2)}) collective-permute-start(bf16[4,8,8,8,128]{4,3,2,1,0:T(8,128)(2,1)} %get-tuple-element.33), channel_id=1, source_target_pairs={{16,0},{17,1},{18,2},{19,3},{20,4},{21,5},{22,6},{23,7},{24,8},{25... | collective-permute-start | bytes 1572872 | tf_op jit(solution)/shard_map/ppermute | solution.py:14
  244.8 98.7 %collective-permute-start.10 = (bf16[4,8,8,8,128]{4,3,2,1,0:T(8,128)(2,1)}, bf16[4,8,8,8,128]{4,3,2,1,0:T(8,128)(2,1)}, u32[]{:S(2)}, u32[]{:S(2)}) collective-permute-start(bf16[4,8,8,8,128]{4,3,2,1,0:T(8,128)(2,1)} %get-tuple-element.32), channel_id=1, source_target_pairs={{15,0},{16,1},{17,2},{18,3},{19,4},{20,5},{21,6},{22,7},{23,8},{24... | collective-permute-start | bytes 1572872 | tf_op jit(solution)/shard_map/ppermute | solution.py:14
  314.4 2.6 copy-start.14
  314.4 12.9 %copy-start.13 = (bf16[4,8,8,8,128]{4,3,2,1,0:T(8,128)(2,1)S(1)}, bf16[4,8,8,8,128]{4,3,2,1,0:T(8,128)(2,1)}, u32[]{:S(2)}) copy-start(bf16[4,8,8,8,128]{4,3,2,1,0:T(8,128)(2,1)} %get-tuple-element.30) | copy-start | bytes 1572868
  314.4 14.8 %copy-start.4 = (bf16[1,1,16,8,8,8,128]{6,2,5,4,3,1,0:T(8,128)(2,1)S(1)}, bf16[1,1,16,8,8,8,128]{6,2,5,4,3,1,0:T(8,128)(2,1)}, u32[]{:S(2)}) copy-start(bf16[1,1,16,8,8,8,128]{6,2,5,4,3,1,0:T(8,128)(2,1)} %get-tuple-element.24) | copy-start | bytes 6291460
  314.9 16.2 %copy-start.12 = (bf16[4,8,8,8,128]{4,3,2,1,0:T(8,128)(2,1)S(1)}, bf16[4,8,8,8,128]{4,3,2,1,0:T(8,128)(2,1)}, u32[]{:S(2)}) copy-start(bf16[4,8,8,8,128]{4,3,2,1,0:T(8,128)(2,1)} %get-tuple-element.29) | copy-start | bytes 1572868
  317.0 22.9 %copy-start.11 = (bf16[4,8,8,8,128]{4,3,2,1,0:T(8,128)(2,1)S(1)}, bf16[4,8,8,8,128]{4,3,2,1,0:T(8,128)(2,1)}, u32[]{:S(2)}) copy-start(bf16[4,8,8,8,128]{4,3,2,1,0:T(8,128)(2,1)} %get-tuple-element.28) | copy-start | bytes 1572868
  317.0 29.3 %collective-permute-start.11 = (bf16[4,8,8,8,128]{4,3,2,1,0:T(8,128)(2,1)S(1)}, bf16[4,8,8,8,128]{4,3,2,1,0:T(8,128)(2,1)S(1)}, u32[]{:S(2)}, u32[]{:S(2)}) collective-permute-start(bf16[4,8,8,8,128]{4,3,2,1,0:T(8,128)(2,1)S(1)} %copy-done.14), channel_id=1, source_target_pairs={{1,0},{2,1},{3,2},{4,3},{5,4},{6,5},{7,6},{8,7},{9,8},{10,9},{11,1... | collective-permute-start | bytes 1572872 | tf_op jit(solution)/shard_map/ppermute | solution.py:14
  327.3 19.1 %collective-permute-start.12 = (bf16[4,8,8,8,128]{4,3,2,1,0:T(8,128)(2,1)S(1)}, bf16[4,8,8,8,128]{4,3,2,1,0:T(8,128)(2,1)S(1)}, u32[]{:S(2)}, u32[]{:S(2)}) collective-permute-start(bf16[4,8,8,8,128]{4,3,2,1,0:T(8,128)(2,1)S(1)} %copy-done.13), channel_id=1, source_target_pairs={{0,1},{1,2},{2,3},{3,4},{4,5},{5,6},{6,7},{7,8},{8,9},{9,10},{10,1... | collective-permute-start | bytes 1572872 | tf_op jit(solution)/shard_map/ppermute | solution.py:14
  331.1 19.3 %collective-permute-start.13 = (bf16[4,8,8,8,128]{4,3,2,1,0:T(8,128)(2,1)S(1)}, bf16[4,8,8,8,128]{4,3,2,1,0:T(8,128)(2,1)S(1)}, u32[]{:S(2)}, u32[]{:S(2)}) collective-permute-start(bf16[4,8,8,8,128]{4,3,2,1,0:T(8,128)(2,1)S(1)} %copy-done.12), channel_id=1, source_target_pairs={{0,15},{1,16},{2,17},{3,18},{4,19},{5,20},{6,21},{7,22},{8,23},{9,... | collective-permute-start | bytes 1572872 | tf_op jit(solution)/shard_map/ppermute | solution.py:14
  339.9 24.6 %collective-permute-start.14 = (bf16[4,8,8,8,128]{4,3,2,1,0:T(8,128)(2,1)S(1)}, bf16[4,8,8,8,128]{4,3,2,1,0:T(8,128)(2,1)S(1)}, u32[]{:S(2)}, u32[]{:S(2)}) collective-permute-start(bf16[4,8,8,8,128]{4,3,2,1,0:T(8,128)(2,1)S(1)} %copy-done.11), channel_id=1, source_target_pairs={{0,16},{1,17},{2,18},{3,19},{4,20},{5,21},{6,22},{7,23},{8,24},{9,... | collective-permute-start | bytes 1572872 | tf_op jit(solution)/shard_map/ppermute | solution.py:14
  343.5 21.2 %collective-permute-start.15 = (bf16[4,8,8,8,128]{4,3,2,1,0:T(8,128)(2,1)S(1)}, bf16[4,8,8,8,128]{4,3,2,1,0:T(8,128)(2,1)S(1)}, u32[]{:S(2)}, u32[]{:S(2)}) collective-permute-start(bf16[4,8,8,8,128]{4,3,2,1,0:T(8,128)(2,1)S(1)} %get-tuple-element.27), channel_id=1, source_target_pairs={{0,17},{1,18},{2,19},{3,20},{4,21},{5,22},{6,23},{7,24},{8,25},{9,... | collective-permute-start | bytes 1572872 | tf_op jit(solution)/shard_map/ppermute | solution.py:14
  367.0 0.7 copy-start.24
  368.2 25.3 %copy-start.7 = (s32[16384]{0:T(1024)S(1)}, s32[16384]{0:T(1024)}, u32[]{:S(2)}) copy-start(s32[16384]{0:T(1024)} %copy-done.6) | copy-start | bytes 196612
  393.5 34.3 %copy-start.16 = (pred[16000]{0:T(1024)(128)(4,1)S(1)}, pred[16000]{0:T(1024)(128)(4,1)}, u32[]{:S(2)}) copy-start(pred[16000]{0:T(1024)(128)(4,1)} %copy-done.15) | copy-start | bytes 48004
Sparse Core Ops, SparseCore 0:
  222.1 83.6 all-reduce.4
  427.9 84.6 all-reduce.6
